TPU v7x, 32 devices: a whole 2x2x4 slice. The times are simulated.
32 devices in a mesh: req: 2 (over y), ctx: 4 (over x, core), tp: 4 (over z).
Axes of the slice: x: 2, y: 2, z: 4, core: 2. Of those that a mesh axis runs over, the one named last changes fastest.
Arguments:
- hidden_in: bfloat16 [4096, 6144], P(('req', 'ctx', 'tp')), parts along dimension 0, may hold values from -5 to 5
- queries: bfloat16 [4096, 4096], P(('req', 'ctx', 'tp')), parts along dimension 0, may hold values from -40 to 40
- keys: bfloat16 [4096, 1024], P(('req', 'ctx', 'tp')), parts along dimension 0, may hold values from -8 to 8
- values: bfloat16 [4096, 1024], P(('req', 'ctx', 'tp')), parts along dimension 0, may hold values from -6 to 6
- block_order: int32 [8], P('req'), parts along dimension 0, may hold values from 0 to 3, each once
- routes: int32 [4096, 2], P(('req', 'ctx')), parts along dimension 0, may hold values from 0 to 7, as said below
- out_weight: bfloat16 [4096, 6144], P('tp'), may hold values from -0.09375 to 0.09375
- norm_gain: float32 [6144], replicated, may hold values from 0.1 to 1.9
- router_weight: bfloat16 [6144, 8], replicated, may hold values from -0.078125 to 0.078125
- gate_weight: bfloat16 [6144, 8192], P(None, 'tp'), may hold values from -0.078125 to 0.078125
- up_weight: bfloat16 [6144, 8192], P(None, 'tp'), may hold values from -0.078125 to 0.078125
- down_weight: bfloat16 [8192, 6144], P('tp'), may hold values from -0.0625 to 0.0625
Outputs:
- attended: bfloat16 [4096, 6144], P(('req', 'ctx', 'tp')), parts along dimension 0
- expert_out: bfloat16 [4096, 6144], P(('req', 'ctx', 'tp')), parts along dimension 0
There are 2 independent parts, one for each index of `req`. A program takes and returns all parts, laid end to end along the dimension named above; an argument that names none is the same for every part. Nothing has to cross between parts.
Inputs may be any that keep to these rules, and one draw needn't show every extreme that they name: `routes`: each row names two different experts. In each block of 512 rows at most 192 rows name expert 0, and exactly 192 in at least one block.
All inputs are finite; a program needn't handle non-finite values.
Results may differ from a plain program's by a relative error of at most 0.023.
Values may be sent and summed in bfloat16 or wider, within the bound.
No kernel may reach another device: no remote copies, remote signals or barrier semaphores. Data moves between devices by JAX's collectives and lax.ppermute only.
A program may use at most 256 MiB of HBM per device.

v0:
```python
import math

import jax
import jax.numpy as jnp
from jax import lax
from jax.sharding import PartitionSpec as P

HEADS = 32
KV_HEADS = 8
HD = 128


def on_device(
    hidden_in,
    queries,
    keys,
    values,
    block_order,
    routes,
    out_weight,
    norm_gain,
    router_weight,
    gate_weight,
    up_weight,
    down_weight,
):
    tensor_width = lax.axis_size("tp")
    local_rows = hidden_in.shape[0]
    block_rows = local_rows * tensor_width
    per_device = HEADS // tensor_width
    grouping = HEADS // KV_HEADS
    repeat_by = max(1, grouping // per_device)
    pairs_device = max(1, per_device // grouping)
    sharing = per_device // pairs_device

    def spread(source):
        widened = jnp.repeat(source.reshape(local_rows, KV_HEADS, HD), repeat_by, axis=1)
        return widened.reshape(local_rows, tensor_width, pairs_device, HD)

    sent_query = queries.reshape(local_rows, tensor_width, per_device * HD)
    sent_pairs = jnp.stack([spread(keys), spread(values)], axis=2).reshape(
        local_rows, tensor_width, 2 * pairs_device * HD
    )
    got_query, got_pairs = (
        lax.all_to_all(sent_query, "tp", split_axis=1, concat_axis=0, tiled=True),
        lax.all_to_all(sent_pairs, "tp", split_axis=1, concat_axis=0, tiled=True),
    )
    query_heads = got_query.reshape(block_rows, pairs_device, sharing, HD)
    local_pairs = got_pairs.reshape(block_rows, 2 * pairs_device * HD)
    context_count = block_order.shape[0]
    context_ids = jnp.arange(context_count, dtype=jnp.int32)
    my_block = jnp.sum(jnp.where(context_ids == lax.axis_index("ctx"), block_order, 0))
    query_place = my_block * block_rows + jnp.arange(block_rows, dtype=jnp.int32)
    factor = 1.0 / math.sqrt(HD)
    piece = lax.all_gather(local_pairs, "ctx", axis=0, tiled=True)
    count = piece.shape[0]
    key_rows = jnp.arange(count, dtype=jnp.int32)
    owner = key_rows // block_rows
    key_place = (
        jnp.sum(jnp.where(owner[:, None] == context_ids[None, :], block_order[None, :], 0), axis=1)
        * block_rows
        + key_rows % block_rows
    )
    key_part = piece[:, : pairs_device * HD].reshape(count, pairs_device, HD)
    value_part = piece[:, pairs_device * HD :].reshape(count, pairs_device, HD)
    highest = jnp.full((pairs_device, sharing, block_rows), -1e30, jnp.float32)
    scores = (
        jnp.einsum("qkgd,nkd->kgqn", query_heads, key_part, preferred_element_type=jnp.float32)
        * factor
    )
    visible = key_place[None, :] <= query_place[:, None]
    scores = jnp.where(visible, scores, -1e30)
    raised = jnp.maximum(highest, jnp.max(scores, axis=-1))
    weights = jnp.where(visible, jnp.exp(scores - raised[..., None]), 0.0)
    norm = jnp.sum(weights, axis=-1)
    probs = weights.astype(jnp.bfloat16)
    accum = jnp.einsum("kgqn,nkd->kgqd", probs, value_part, preferred_element_type=jnp.float32)
    highest, norm, accum = (raised, norm, accum)
    heads_out = (
        (accum / norm[..., None])
        .transpose(2, 0, 1, 3)
        .reshape(block_rows, per_device * HD)
        .astype(jnp.bfloat16)
    )
    head_sum = lax.psum_scatter(
        jnp.dot(heads_out, out_weight, preferred_element_type=jnp.float32).astype(jnp.bfloat16),
        "tp",
        scatter_dimension=0,
        tiled=True,
    ).astype(jnp.float32)
    attended = (hidden_in.astype(jnp.float32) + head_sum).astype(jnp.bfloat16)
    widened = attended.astype(jnp.float32)
    normed = (
        widened * lax.rsqrt(jnp.mean(widened * widened, axis=1, keepdims=True) + 1e-05) * norm_gain
    ).astype(jnp.bfloat16)
    expert_ids = jnp.arange(router_weight.shape[1], dtype=jnp.int32)
    piece = lax.all_gather(normed, "tp", axis=0, tiled=True)
    logits = jnp.dot(piece, router_weight, preferred_element_type=jnp.float32)
    first = jnp.sum(jnp.where(routes[:, 0:1] == expert_ids[None, :], logits, 0.0), axis=1)
    second = jnp.sum(jnp.where(routes[:, 1:2] == expert_ids[None, :], logits, 0.0), axis=1)
    share = jnp.where(routes[:, 0] == 0, 1.0 / (1.0 + jnp.exp(second - first)), 0.0)
    activate_share = share + jnp.where(
        routes[:, 1] == 0, 1.0 / (1.0 + jnp.exp(first - second)), 0.0
    )
    gate = jnp.dot(piece, gate_weight, preferred_element_type=jnp.float32)
    upward = jnp.dot(piece, up_weight, preferred_element_type=jnp.float32)
    acts = (jax.nn.silu(gate) * upward * activate_share[:, None]).astype(jnp.bfloat16)
    expert_out = lax.psum_scatter(
        jnp.dot(acts, down_weight, preferred_element_type=jnp.float32).astype(jnp.bfloat16),
        "tp",
        scatter_dimension=0,
        tiled=True,
    )
    return (attended, expert_out)


def solution(mesh):
    return jax.shard_map(
        on_device,
        mesh=mesh,
        in_specs=(
            P(("req", "ctx", "tp"), None),
            P(("req", "ctx", "tp"), None),
            P(("req", "ctx", "tp"), None),
            P(("req", "ctx", "tp"), None),
            P("req"),
            P(("req", "ctx"), None),
            P("tp", None),
            P(),
            P(),
            P(None, "tp"),
            P(None, "tp"),
            P("tp", None),
        ),
        out_specs=(P(("req", "ctx", "tp"), None), P(("req", "ctx", "tp"), None)),
        check_vma=False,
    )
```

profile of v0, /device:TPU:0, one launch (start us, length us, event | category | flops | bytes accessed | tf_op | source)
XLA Modules:
  0.0 534.1 jit_solution(314289920556781188)
XLA Ops:
  7.2 0.0 all-gather.3.cloned.1.call-start
  7.2 1.1 copy.31
  8.4 1.1 copy.30
  9.5 0.1 pad_maximum_fusion
  9.5 20.6 %all_to_all.30 = bf16[128,4,512]{0,2,1:T(8,128)(2,1)S(1)} all-to-all(bf16[128,4,512]{0,2,1:T(8,128)(2,1)S(1)} %bitcast.66), channel_id=1, replica_groups=mesh['req'=2,'ctx'=4,'tp'=4] {'tp'}, dimensions={1} | all-to-all | bytes 1048576 | tf_op jit(solution)/shard_map/all_to_all | solution.py:46
  30.2 1.0 copy.32
  31.2 2.3 copy.50
  33.5 3.5 all-to-all-start.1
  37.0 0.0 reduce-scatter.3.cloned.1.call-start
  37.1 0.6 fusion.23
  38.4 0.1 select_reduce_fusion
  38.5 0.8 broadcast_compare_fusion
  39.3 22.6 %all-to-all-done.1 = bf16[128,4,1024]{2,0,1:T(8,128)(2,1)S(1)} async-done(((bf16[128,4,1024]{2,0,1:T(8,128)(2,1)}), bf16[128,4,1024]{2,0,1:T(8,128)(2,1)S(1)}, u32[]{:S(2)}, u32[]{:S(2)}) %all-to-all-start.1) | async-done | bytes 1048608 | tf_op jit(solution)/shard_map/all_to_all | solution.py:45
  61.8 1.5 reshape.124
  63.4 1.7 fusion.27
  65.0 1.4 copy.37
  66.5 0.6 copy.33
  67.1 15.1 %fusion = (f32[2,4,512]{2,1,0:T(4,128)S(1)}, f32[2,2048,512,4]{2,1,3,0:T(8,128)}) fusion(pred[512,2048]{0,1:T(8,128)(4,1)S(1)} %broadcast_compare_fusion, bf16[2048,2,128,1]{0,2,3,1:T(8,128)(2,1)S(1)} %bitcast.70, bf16[512,2,4,128]{3,2,1,0:T(4,128)(2,1)} %reshape.124), kind=kOutput, calls=%fused_computation.2 | convolution fusion | flops 2172645376 | bytes 36716544 | tf_op jit(solution)/shard_map/qkgd,nkd->kgqn/dot_general | solution.py:68
  82.3 15.0 %fusion.1 = f32[2,4,512]{2,1,0:T(4,128)S(1)} fusion(f32[2,2048,512,4]{2,1,3,0:T(8,128)} %get-tuple-element.13, f32[2,4,512]{2,1,0:T(4,128)S(1)} %broadcast_maximum_fusion, pred[512,2048]{0,1:T(8,128)(4,1)S(1)} %broadcast_compare_fusion), kind=kLoop, calls=%fused_computation.3 | loop fusion | flops 41938944 | bytes 34635776 | tf_op jit(solution)/shard_map/reduce_sum | solution.py:75
  97.3 14.7 %fusion.9 = bf16[512,2,4,128]{0,3,2,1:T(8,128)(2,1)S(1)} fusion(bf16[2048,2,128,1]{0,2,3,1:T(8,128)(2,1)S(1)} %bitcast.69, f32[2,2048,512,4]{2,1,3,0:T(8,128)} %get-tuple-element.13, f32[2,4,512]{2,1,0:T(4,128)S(1)} %broadcast_maximum_fusion, pred[512,2048]{0,1:T(8,128)(4,1)S(1)} %broadcast_compare_fusion, f32[512,2,4]{0,2,1:T(4,128)S(1)} %bitcast.75), kind=kOutput, calls=%fused_computation.17 | convolution fusion | flops 2190475264 | bytes 36732928 | tf_op jit(solution)/shard_map/kgqn,nkd->kgqd/dot_general | solution.py:77
  112.0 13.3 %convolution_convert_fusion.1 = bf16[512,6144]{1,0:T(8,128)(2,1)} fusion(bf16[512,1024]{0,1:T(8,128)(2,1)S(1)} %bitcast.79, bf16[1024,6144]{1,0:T(8,128)(2,1)} %param.18), kind=kOutput, calls=%fused_computation.8 | convolution fusion | flops 6445596672 | bytes 19922944 | tf_op jit(solution)/shard_map/dot_general | solution.py:86
  125.3 0.2 all-gather.5.cloned.1.call-start
  125.5 109.8 %reduce-scatter.3.cloned.1.call-done = bf16[128,6144]{1,0:T(8,128)(2,1)} async-done(((bf16[512,6144]{1,0:T(8,128)(2,1)}), bf16[128,6144]{1,0:T(8,128)(2,1)}) %reduce-scatter.3.cloned.1.call-update) | async-done | bytes 1572880 | tf_op jit(solution)/shard_map/reduce_scatter | solution.py:85
  235.3 2.0 fusion.6
  237.4 1.6 fusion.8
  239.1 0.0 reduce-scatter.5.cloned.1.call-start
  239.1 116.0 %all-gather.5.cloned.1.call-done = bf16[512,6144]{1,0:T(8,128)(2,1)} async-done(((bf16[128,6144]{1,0:T(8,128)(2,1)}), bf16[512,6144]{1,0:T(8,128)(2,1)}) %all-gather.5.cloned.1.call-update) | async-done | bytes 6291472 | tf_op jit(solution)/shard_map/all_gather | solution.py:97
  355.1 4.7 select_reduce_fusion.1
  359.8 19.5 %fusion.29 = f32[512,2048]{1,0:T(8,128)} fusion(bf16[512,6144]{1,0:T(8,128)(2,1)S(1)} %copy-done.3, bf16[6144,2048]{1,0:T(8,128)(2,1)} %param.21), kind=kOutput, calls=%fused_computation.56 | convolution fusion | flops 12884901888 | bytes 35651584 | tf_op jit(solution)/shard_map/dot_general | solution.py:105
  379.3 19.1 %multiply_convert_fusion = bf16[512,2048]{1,0:T(8,128)(2,1)S(1)} fusion(f32[512,2048]{1,0:T(8,128)} %fusion.29, bf16[512,6144]{1,0:T(8,128)(2,1)S(1)} %copy-done.3, bf16[6144,2048]{1,0:T(8,128)(2,1)} %param.22, f32[512]{0:T(512)S(1)} %bitcast.78), kind=kOutput, calls=%fused_computation.9 | convolution fusion | flops 12892241920 | bytes 37750784 | tf_op jit(solution)/shard_map/dot_general | solution.py:106
  398.5 19.9 %convolution_convert_fusion = bf16[512,6144]{1,0:T(8,128)(2,1)} fusion(bf16[512,2048]{1,0:T(8,128)(2,1)S(1)} %multiply_convert_fusion, bf16[2048,6144]{1,0:T(8,128)(2,1)} %param.23), kind=kOutput, calls=%fused_computation.7 | convolution fusion | flops 12888047616 | bytes 33554432 | tf_op jit(solution)/shard_map/dot_general | solution.py:109
  418.4 109.1 %reduce-scatter.5.cloned.1.call-done = bf16[128,6144]{1,0:T(8,128)(2,1)} async-done(((bf16[512,6144]{1,0:T(8,128)(2,1)}), bf16[128,6144]{1,0:T(8,128)(2,1)}) %reduce-scatter.5.cloned.1.call-update) | async-done | bytes 1572880 | tf_op jit(solution)/shard_map/reduce_scatter | solution.py:108
  (31 shorter events, 0.2 us)
Async XLA Ops:
  7.2 347.9 %copy-start = (bf16[6144,8]{0,1:T(8,128)(2,1)S(1)}, bf16[6144,8]{0,1:T(8,128)(2,1)}, u32[]{:S(2)}) copy-start(bf16[6144,8]{0,1:T(8,128)(2,1)} %param.20) | copy-start | bytes 294916
  7.2 29.9 %copy-start.8 = (s32[4]{0:T(128)S(1)}, s32[4]{0:T(128)}, u32[]{:S(2)}) copy-start(s32[4]{0:T(128)} %param.16) | copy-start | bytes 52
  7.2 56.2 %all-gather.3.cloned.1.call-start = ((), (), s32[]{:S(2)}) async-start(), calls=%async_computation.4 | async-start | bytes 2621440 | tf_op jit(solution)/shard_map/all_gather | solution.py:55
  33.5 28.4 %all-to-all-start.1 = ((bf16[128,4,1024]{2,0,1:T(8,128)(2,1)}), bf16[128,4,1024]{2,0,1:T(8,128)(2,1)S(1)}, u32[]{:S(2)}, u32[]{:S(2)}) async-start(bf16[128,4,1024]{2,0,1:T(8,128)(2,1)} %bitcast.63), calls=%async_computation.1 | async-start | bytes 2097152 | tf_op jit(solution)/shard_map/all_to_all | solution.py:45
  37.0 198.3 %reduce-scatter.3.cloned.1.call-start = ((), (), s32[]{:S(2)}) async-start(), calls=%async_computation.5 | async-start | bytes 7864320 | tf_op jit(solution)/shard_map/reduce_scatter | solution.py:85
  82.3 15.0 %copy-start.5 = (bf16[2048,256]{0,1:T(8,128)(2,1)S(1)}, bf16[2048,256]{0,1:T(8,128)(2,1)}, u32[]{:S(2)}) copy-start(bf16[2048,256]{0,1:T(8,128)(2,1)} %copy.37) | copy-start | bytes 3145732
  125.3 110.0 %copy-start.4 = (bf16[128,6144]{1,0:T(8,128)(2,1)S(1)}, bf16[128,6144]{1,0:T(8,128)(2,1)}, u32[]{:S(2)}) copy-start(bf16[128,6144]{1,0:T(8,128)(2,1)} %param.12) | copy-start | bytes 4718596
  125.3 112.1 %copy-start.6 = (f32[6144]{0:T(1024)S(1)}, f32[6144]{0:T(1024)}, u32[]{:S(2)}) copy-start(f32[6144]{0:T(1024)} %param.19) | copy-start | bytes 73732
  125.3 113.8 %copy-start.7 = (s32[512,2]{0,1:T(2,128)S(1)}, s32[512,2]{0,1:T(2,128)}, u32[]{:S(2)}) copy-start(s32[512,2]{0,1:T(2,128)} %param.17) | copy-start | bytes 12292
  125.3 229.8 %all-gather.5.cloned.1.call-start = ((), (), s32[]{:S(2)}) async-start(), calls=%async_computation.6 | async-start | bytes 7864320 | tf_op jit(solution)/shard_map/all_gather | solution.py:97
  237.4 142.0 %copy-start.2 = (bf16[128,6144]{1,0:T(8,128)(2,1)}, bf16[128,6144]{1,0:T(8,128)(2,1)S(1)}, u32[]{:S(2)}) copy-start(bf16[128,6144]{1,0:T(8,128)(2,1)S(1)} %get-tuple-element.5) | copy-start | bytes 4718596
  239.1 288.5 %reduce-scatter.5.cloned.1.call-start = ((), (), s32[]{:S(2)}) async-start(), calls=%async_computation.7 | async-start | bytes 7864320 | tf_op jit(solution)/shard_map/reduce_scatter | solution.py:108
  355.1 4.7 copy-start.3
  398.5 129.1 %copy-start.1 = (bf16[6144,8]{0,1:T(8,128)(2,1)S(1)}, bf16[6144,8]{0,1:T(8,128)(2,1)}, u32[]{:S(2)}) copy-start(bf16[6144,8]{0,1:T(8,128)(2,1)} %param.20) | copy-start | bytes 294916
Sparse Core Ops, SparseCore 0:
  31.3 21.6 all-gather.2
  125.4 109.8 reduce-scatter.2
  239.2 115.8 all-gather.4
  418.5 108.9 reduce-scatter.4
where the time goes:
time: 535 us; the launch traced here: 534 us
  waiting for transfers between devices  357 us (67%)
  matrix products  106 us (20%)
  blocking collectives  20.6 us (4%)
  other arithmetic  20.2 us (4%)
  between operations  14.7 us (3%)
  local copies, waits for them, and re-layouts  10.9 us (2%)
    all_gather x1, waiting for transfers between devices, on_device(): piece = lax.all_gather(normed, 'tp', axis=0, tiled=True)  116 us
    reduce_scatter x1, waiting for transfers between devices, on_device(): lax.psum_scatter(jnp.dot(heads_out, out_weight, preferred_element_type=jn...  110 us
    reduce_scatter x1, waiting for transfers between devices, on_device(): lax.psum_scatter(jnp.dot(acts, down_weight, preferred_element_type=jnp.fl...  109 us
    all_to_all x1, waiting for transfers between devices, on_device(): lax.all_to_all(sent_query, 'tp', split_axis=1, concat_axis=0, tiled=True)  22.6 us
    all_to_all x1, blocking collectives, on_device(): lax.all_to_all(sent_pairs, 'tp', split_axis=1, concat_axis=0, tiled=True)  20.6 us
    dot_general x1, matrix products, on_device(): jnp.dot(acts, down_weight, preferred_element_type=jnp.float32)  19.9 us
    dot_general x1, matrix products, on_device(): gate = jnp.dot(piece, gate_weight, preferred_element_type=jnp.float32)  19.5 us
    dot_general x1, matrix products, on_device(): upward = jnp.dot(piece, up_weight, preferred_element_type=jnp.float32)  19.1 us
  transfers between devices with their start and end apart: 5, of which 4 were waited for; matrix products, arithmetic and copies ran while one was open for 1% of the time, Pallas kernels for 0%

commit v1 on v0

v1 whole, which is shorter than its diff:
```python
import functools
import math

import jax
import jax.numpy as jnp
from jax import lax
from jax.experimental import pallas as pl
from jax.experimental.pallas import tpu as pltpu
from jax.sharding import PartitionSpec as P

HEADS = 32
KV_HEADS = 8
HD = 128
FACTOR = math.log2(math.e) / math.sqrt(HD)


def attention_kernel(pairs, sharing, block_rows, info, q_ref, place_ref, kv_ref, out_ref):
    half = q_ref.shape[1]
    tall = sharing * half
    my_block = info[0]
    place = jnp.concatenate([place_ref[0]] * sharing, axis=0)
    ones = jnp.ones((block_rows, HD), jnp.bfloat16)
    queries = []
    for p in range(pairs):
        heads = [q_ref[0, :, (p * sharing + g) * HD : (p * sharing + g + 1) * HD] for g in range(sharing)]
        queries.append(jnp.concatenate(heads, axis=0))

    def scores_of(p, start):
        key = kv_ref[pl.ds(start, block_rows), p * HD : (p + 1) * HD]
        return lax.dot_general(queries[p], key, (((1,), (1,)), ((), ())), preferred_element_type=jnp.float32)

    def mixed_of(p, start, weights):
        value = kv_ref[pl.ds(start, block_rows), (pairs + p) * HD : (pairs + p + 1) * HD]
        return jnp.dot(weights, jnp.concatenate([value, ones], axis=1), preferred_element_type=jnp.float32)

    def start_of(place_in_prompt):
        return pl.multiple_of(info[1 + place_in_prompt] * block_rows, block_rows)

    own = start_of(my_block)
    key_place = lax.broadcasted_iota(jnp.int32, (tall, block_rows), 1)
    state = []
    for p in range(pairs):
        scores = jnp.where(key_place <= place, scores_of(p, own), -1e30)
        top = jnp.max(scores, axis=1, keepdims=True)
        weights = jnp.exp2((scores - top) * FACTOR).astype(jnp.bfloat16)
        state.append((top, mixed_of(p, own, weights)))

    def earlier(step, state):
        start = start_of(step)
        new = []
        for p in range(pairs):
            top, total = state[p]
            scores = scores_of(p, start)
            raised = jnp.maximum(top, jnp.max(scores, axis=1, keepdims=True))
            weights = jnp.exp2((scores - raised) * FACTOR).astype(jnp.bfloat16)
            total = total * jnp.exp2((top - raised) * FACTOR) + mixed_of(p, start, weights)
            new.append((raised, total))
        return new

    state = lax.fori_loop(0, my_block, earlier, state)
    for p in range(pairs):
        total = state[p][1]
        mixed = (total[:, :HD] / total[:, HD:]).astype(jnp.bfloat16)
        for g in range(sharing):
            at = (p * sharing + g) * HD
            out_ref[0, :, at : at + HD] = mixed[g * half : (g + 1) * half]


def attend(info, queries, places, pairs_all, which, half, pairs, sharing, block_rows):
    shards, _, width = queries.shape
    count = pairs_all.shape[0]
    flops = 4 * shards * half * width * count
    return pl.pallas_call(
        functools.partial(attention_kernel, pairs, sharing, block_rows),
        grid_spec=pltpu.PrefetchScalarGridSpec(
            num_scalar_prefetch=1,
            grid=(shards,),
            in_specs=[
                pl.BlockSpec((1, half, width), lambda s, info: (s, which, 0)),
                pl.BlockSpec((1, half, 1), lambda s, info: (s, which, 0)),
                pl.BlockSpec(pairs_all.shape, lambda s, info: (0, 0)),
            ],
            out_specs=pl.BlockSpec((1, half, width), lambda s, info: (s, 0, 0)),
        ),
        out_shape=jax.ShapeDtypeStruct((shards, half, width), jnp.bfloat16),
        compiler_params=pltpu.CompilerParams(vmem_limit_bytes=24 * 1024 * 1024),
        cost_estimate=pl.CostEstimate(
            flops=flops,
            bytes_accessed=2 * (2 * shards * half * width + pairs_all.size),
            transcendentals=shards * half * width // HD * count,
        ),
    )(info, queries, places, pairs_all)


def on_device(
    hidden_in,
    queries,
    keys,
    values,
    block_order,
    routes,
    out_weight,
    norm_gain,
    router_weight,
    gate_weight,
    up_weight,
    down_weight,
):
    shards = lax.axis_size("tp")
    rows = hidden_in.shape[0]
    block_rows = rows * shards
    per_device = HEADS // shards
    grouping = HEADS // KV_HEADS
    repeat_by = max(1, grouping // per_device)
    pairs = max(1, per_device // grouping)
    sharing = per_device // pairs
    half = rows // 2 if rows % 32 == 0 else rows
    halves = rows // half

    def spread(source):
        widened = jnp.repeat(source.reshape(rows, KV_HEADS, HD), repeat_by, axis=1)
        return widened.reshape(rows, shards, pairs, HD)

    sent_pairs = jnp.stack([spread(keys), spread(values)], axis=2).reshape(rows, shards, 2 * pairs * HD)
    got_pairs = lax.all_to_all(sent_pairs, "tp", split_axis=1, concat_axis=0, tiled=True)
    pairs_all = lax.all_gather(got_pairs.reshape(block_rows, 2 * pairs * HD), "ctx", axis=0, tiled=True)

    picked = ((routes[:, 0] == 0) | (routes[:, 1] == 0)).reshape(shards, rows)
    row_ids = jnp.arange(rows, dtype=jnp.int32)
    up_to = (row_ids[:, None] <= row_ids[None, :]).astype(jnp.bfloat16)
    seen = jnp.dot(picked.astype(jnp.bfloat16), up_to, preferred_element_type=jnp.float32).astype(jnp.int32)
    count = seen[:, -1:]
    slot = jnp.where(picked, seen - 1, count + row_ids[None, :] - seen)
    fullest = lax.pmax(jnp.max(count), ("req", "ctx"))
    at_slot = slot[:, None, :] == row_ids[None, :, None]
    row_of_slot = jnp.sum(jnp.where(at_slot, row_ids[None, None, :], 0), axis=2)
    places = (row_of_slot + jnp.arange(shards, dtype=jnp.int32)[:, None] * rows)[:, :, None]
    me = lax.axis_index("tp")
    my_slot = lax.dynamic_index_in_dim(slot, me, 0, keepdims=False)
    order = (my_slot[None, :] == row_ids[:, None]).astype(jnp.bfloat16)

    def reorder(source):
        return jnp.dot(order, source, preferred_element_type=jnp.float32).astype(jnp.bfloat16)

    def restore(parts):
        whole = jnp.concatenate(parts, axis=0) if len(parts) > 1 else parts[0]
        return lax.dot_general(
            order, whole, (((0,), (0,)), ((), ())), preferred_element_type=jnp.float32
        ).astype(jnp.bfloat16)

    sent_query = reorder(queries).reshape(rows, shards, per_device * HD)
    got_query = lax.all_to_all(sent_query, "tp", split_axis=1, concat_axis=0, tiled=True)
    got_query = got_query.reshape(shards, rows, per_device * HD)

    ctx_ids = jnp.arange(block_order.shape[0], dtype=jnp.int32)
    my_block = jnp.sum(jnp.where(ctx_ids == lax.axis_index("ctx"), block_order, 0))
    holder = jnp.sum(jnp.where(block_order[None, :] == ctx_ids[:, None], ctx_ids[None, :], 0), axis=1)
    info = jnp.concatenate([my_block[None], holder])

    hidden = reorder(hidden_in).astype(jnp.float32)
    my_routes = lax.dynamic_slice_in_dim(routes, me * rows, rows, 0)
    my_routes = jnp.sum(
        jnp.where((my_slot[None, :] == row_ids[:, None])[:, :, None], my_routes[None, :, :], 0), axis=1
    )
    expert_ids = jnp.arange(router_weight.shape[1], dtype=jnp.int32)

    def project(which):
        heads = attend(info, got_query, places, pairs_all, which, half, pairs, sharing, block_rows)
        heads = heads.reshape(shards * half, per_device * HD)
        return jnp.dot(heads, out_weight, preferred_element_type=jnp.float32).astype(jnp.bfloat16)

    def gather_sum(term):
        return lax.psum_scatter(term, "tp", scatter_dimension=0, tiled=True)

    def finish(which, head_sum):
        return (hidden[which * half : (which + 1) * half] + head_sum.astype(jnp.float32)).astype(jnp.bfloat16)

    def expert(which, attended):
        widened = attended.astype(jnp.float32)
        normed = (
            widened * lax.rsqrt(jnp.mean(widened * widened, axis=1, keepdims=True) + 1e-05) * norm_gain
        ).astype(jnp.bfloat16)
        chosen = lax.all_gather(normed, "tp", axis=0, tiled=True)
        logits = jnp.dot(normed, router_weight, preferred_element_type=jnp.float32)
        slots = my_routes[which * half : (which + 1) * half]
        first = jnp.sum(jnp.where(slots[:, 0:1] == expert_ids[None, :], logits, 0.0), axis=1)
        second = jnp.sum(jnp.where(slots[:, 1:2] == expert_ids[None, :], logits, 0.0), axis=1)
        share = jnp.where(slots[:, 0] == 0, 1.0 / (1.0 + jnp.exp(second - first)), 0.0)
        share = share + jnp.where(slots[:, 1] == 0, 1.0 / (1.0 + jnp.exp(first - second)), 0.0)
        gate = jnp.dot(chosen, gate_weight, preferred_element_type=jnp.float32)
        upward = jnp.dot(chosen, up_weight, preferred_element_type=jnp.float32)
        acts = (jax.nn.silu(gate) * upward).astype(jnp.bfloat16)
        total = gather_sum(jnp.dot(acts, down_weight, preferred_element_type=jnp.float32).astype(jnp.bfloat16))
        return (total.astype(jnp.float32) * share[:, None]).astype(jnp.bfloat16)

    attended = [finish(0, gather_sum(project(0)))]
    experts = [expert(0, attended[0])]
    if halves > 1:
        attended.append(finish(1, gather_sum(project(1))))
        experts.append(
            lax.cond(
                fullest > half,
                lambda source: expert(1, source),
                jnp.zeros_like,
                attended[1],
            )
        )
    return (restore(attended), restore(experts))


def solution(mesh):
    return jax.shard_map(
        on_device,
        mesh=mesh,
        in_specs=(
            P(("req", "ctx", "tp"), None),
            P(("req", "ctx", "tp"), None),
            P(("req", "ctx", "tp"), None),
            P(("req", "ctx", "tp"), None),
            P("req"),
            P(("req", "ctx"), None),
            P("tp", None),
            P(),
            P(),
            P(None, "tp"),
            P(None, "tp"),
            P("tp", None),
        ),
        out_specs=(P(("req", "ctx", "tp"), None), P(("req", "ctx", "tp"), None)),
        check_vma=False,
    )
```

time: 535 us -> 390 us (0.73)
  waiting for transfers between devices: 357 us -> 231 us
  matrix products: 106 us -> 65.1 us
  Pallas kernels: 0 us -> 20.6 us
  blocking collectives: 20.6 us -> 35.6 us
  other arithmetic: 20.2 us -> 8.66 us
    reduce_scatter x2 -> x3, waiting for transfers between devices: 219 us -> 142 us  [gather_sum(): return lax.psum_scatter(term, 'tp', scatter_dimension=0, tiled=True)]
    all_gather x2, waiting for transfers between devices: 116 us -> 65.6 us  [the longest x1 65.6 us: expert(): chosen = lax.all_gather(normed, 'tp', axis=0, tiled=True)]
    dot_general x7 -> x10, matrix products: 106 us -> 65.1 us  [the longest x1 23.8 us: expert(): jnp.dot(acts, down_weight, preferred_element_type=jnp.float32)]
    pallas_call x0 -> x2, Pallas kernels: none -> 20.6 us  [attend(): pl.pallas_call(functools.partial(attention_kernel, pairs, sharing, block_...]
    pmax x0 -> x1, blocking collectives: none -> 14.9 us  [on_device(): fullest = lax.pmax(jnp.max(count), ('req', 'ctx'))]
    reduce_sum x4 -> x5, other arithmetic: 17.7 us -> 3.8 us  [the longest x1 2.8 us: expert(): jnp.mean(widened * widened, axis=1, keepdims=True) + 1e-05]
  transfers between devices with their start and end apart: 5 -> 6, of which waited for: 4 -> 5; matrix products, arithmetic and copies ran while one was open for 1% -> 6% of each run, Pallas kernels for 0% -> 3%
where the time goes in v1:
time: 390 us
  waiting for transfers between devices  231 us (59%)
  matrix products  65.1 us (17%)
  blocking collectives  35.6 us (9%)
  Pallas kernels  20.6 us (5%)
  between operations  14.7 us (4%)
  local copies, waits for them, and re-layouts  11 us (3%)
  other arithmetic  8.66 us (2%)
    reduce_scatter x3, waiting for transfers between devices, gather_sum(): return lax.psum_scatter(term, 'tp', scatter_dimension=0, tiled=True)  142 us
    all_gather x1, waiting for transfers between devices, expert(): chosen = lax.all_gather(normed, 'tp', axis=0, tiled=True)  65.6 us
    dot_general x1, matrix products, expert(): jnp.dot(acts, down_weight, preferred_element_type=jnp.float32)  23.8 us
    all_to_all x1, waiting for transfers between devices, on_device(): lax.all_to_all(sent_query, 'tp', split_axis=1, concat_axis=0, tiled=True)  22.9 us
    all_to_all x1, blocking collectives, on_device(): lax.all_to_all(sent_pairs, 'tp', split_axis=1, concat_axis=0, tiled=True)  20.7 us
    pallas_call x2, Pallas kernels, attend(): pl.pallas_call(functools.partial(attention_kernel, pairs, sharing, block_...  20.6 us
    dot_general x2, matrix products, project(): jnp.dot(heads, out_weight, preferred_element_type=jnp.float32)  18.9 us
    pmax x1, blocking collectives, on_device(): fullest = lax.pmax(jnp.max(count), ('req', 'ctx'))  14.9 us
  transfers between devices with their start and end apart: 6, of which 5 were waited for; matrix products, arithmetic and copies ran while one was open for 6% of the time, Pallas kernels for 3%

profile of v1, /device:TPU:0, one launch (start us, length us, event | category | flops | bytes accessed | tf_op | source)
XLA Modules:
  0.0 390.5 jit_solution(9247937463418808739)
XLA Ops:
  7.2 1.2 stack_reshape_reshape_broadcast_in_dim_reshape.6
  8.5 1.1 stack_reshape_reshape_broadcast_in_dim_reshape.7
  9.6 0.7 pad_maximum_fusion
  10.9 20.7 %all_to_all.30 = bf16[128,4,512]{2,0,1:T(8,128)(2,1)} all-to-all(bf16[128,4,512]{2,0,1:T(8,128)(2,1)S(1)} %reshape.209), channel_id=1, replica_groups=mesh['req'=2,'ctx'=4,'tp'=4] {'tp'}, dimensions={1} | all-to-all | bytes 1048576 | tf_op jit(solution)/shard_map/all_to_all | solution.py:125
  31.8 0.7 slice_reduce_fusion
  32.6 1.6 convolution_convert_fusion.7
  34.3 1.3 copy.21
  35.6 2.3 copy.22
  37.9 3.5 all-to-all-start
  41.9 0.6 fusion.37
  42.5 0.7 pad_add_fusion.info
  43.3 22.9 %all-to-all-done = bf16[128,4,1024]{2,0,1:T(8,128)(2,1)S(1)} async-done(((bf16[128,4,1024]{2,0,1:T(8,128)(2,1)}), bf16[128,4,1024]{2,0,1:T(8,128)(2,1)S(1)}, u32[]{:S(2)}, u32[]{:S(2)}) %all-to-all-start) | async-done | bytes 1048608 | tf_op jit(solution)/shard_map/all_to_all | solution.py:152
  66.3 1.6 copy-done.2
  67.9 10.3 %shard_map.132 = bf16[4,64,1024]{2,1,0:T(8,128)(2,1)S(1)} custom-call(s32[5]{0:T(128)S(1)} %pad_add_fusion.info, bf16[4,128,1024]{2,1,0:T(8,128)(2,1)S(1)} %bitcast.71, s32[4,128,1]{2,1,0:T(8,128)S(1)} %broadcast_add_fusion.place_ref, bf16[2048,512]{1,0:T(8,128)(2,1)S(1)} %copy-done.2), custom_call_target="tpu_custom_call" | custom-call | flops 2147483648 | bytes 3145728 | tf_op jit(solution)/shard_map/pallas_call | solution.py:73
  78.2 9.4 %convolution_convert_fusion.2 = bf16[256,6144]{1,0:T(8,128)(2,1)} fusion(bf16[256,1024]{1,0:T(8,128)(2,1)S(1)} %bitcast.74, bf16[1024,6144]{1,0:T(8,128)(2,1)} %param.20), kind=kOutput, calls=%fused_computation.26 | convolution fusion | flops 3222798336 | bytes 16252928 | tf_op jit(solution)/shard_map/dot_general | solution.py:170
  87.7 1.6 copy-done.3
  89.3 10.3 %shard_map.131 = bf16[4,64,1024]{2,1,0:T(8,128)(2,1)S(1)} custom-call(s32[5]{0:T(128)S(1)} %pad_add_fusion.info, bf16[4,128,1024]{2,1,0:T(8,128)(2,1)S(1)} %bitcast.72, s32[4,128,1]{2,1,0:T(8,128)S(1)} %broadcast_add_fusion.place_ref, bf16[2048,512]{1,0:T(8,128)(2,1)S(1)} %copy-done.3), custom_call_target="tpu_custom_call" | custom-call | flops 2147483648 | bytes 3145728 | tf_op jit(solution)/shard_map/pallas_call | solution.py:73
  99.6 9.5 %convolution_convert_fusion.3 = bf16[256,6144]{1,0:T(8,128)(2,1)} fusion(bf16[256,1024]{1,0:T(8,128)(2,1)S(1)} %bitcast.73, bf16[1024,6144]{1,0:T(8,128)(2,1)} %param.20), kind=kOutput, calls=%fused_computation.27 | convolution fusion | flops 3222798336 | bytes 16252928 | tf_op jit(solution)/shard_map/dot_general | solution.py:170
  109.1 14.9 %pmax.7 = s32[]{:T(128)} all-reduce(s32[]{:T(128)} %get-tuple-element.35), channel_id=1, replica_groups=mesh['req'=2,'ctx'=4,'tp'=4] {'req','ctx'}, use_global_device_ids=true, to_apply=%region_11.12 | all-reduce | flops 1 | bytes 8 | tf_op jit(solution)/shard_map/pmax | solution.py:134
  124.8 2.3 fusion.13
  127.0 23.2 %reduce-scatter.9.cloned.1.call-done = bf16[64,6144]{1,0:T(8,128)(2,1)} async-done(((bf16[256,6144]{1,0:T(8,128)(2,1)}), bf16[64,6144]{1,0:T(8,128)(2,1)}) %reduce-scatter.9.cloned.1.call-update) | async-done | bytes 786448 | tf_op jit(solution)/shard_map/reduce_scatter | solution.py:173
  150.3 62.6 %reduce-scatter.7.cloned.1.call-done = bf16[64,6144]{1,0:T(8,128)(2,1)} async-done(((bf16[256,6144]{1,0:T(8,128)(2,1)}), bf16[64,6144]{1,0:T(8,128)(2,1)}) %reduce-scatter.7.cloned.1.call-update) | async-done | bytes 786448 | tf_op jit(solution)/shard_map/reduce_scatter | solution.py:173
  212.9 2.8 fusion.20
  215.7 1.1 fusion.22
  217.8 65.6 %all-gather.8.cloned.1.call-done = bf16[256,6144]{1,0:T(8,128)(2,1)} async-done(((bf16[64,6144]{1,0:T(8,128)(2,1)}), bf16[256,6144]{1,0:T(8,128)(2,1)}) %all-gather.8.cloned.1.call-update) | async-done | bytes 3145744 | tf_op jit(solution)/shard_map/all_gather | solution.py:183
  283.4 13.4 %fusion.45 = f32[256,2048]{1,0:T(8,128)} fusion(bf16[256,6144]{1,0:T(8,128)(2,1)} %all-gather.8.cloned.1.call-done, bf16[6144,2048]{1,0:T(8,128)(2,1)} %param.23), kind=kOutput, calls=%fused_computation.97 | convolution fusion | flops 6442450944 | bytes 30408704 | tf_op jit(solution)/shard_map/dot_general | solution.py:190
  296.8 23.8 %convolution_convert_fusion.1 = bf16[256,6144]{1,0:T(8,128)(2,1)} fusion(bf16[2048,6144]{1,0:T(8,128)(2,1)} %param.25, bf16[256,6144]{1,0:T(8,128)(2,1)} %all-gather.8.cloned.1.call-done, bf16[6144,2048]{1,0:T(8,128)(2,1)} %param.24, f32[256,2048]{1,0:T(8,128)} %fusion.45), kind=kOutput, calls=%fused_computation.25 | convolution fusion | flops 12889620480 | bytes 58720256 | tf_op jit(solution)/shard_map/dot_general | solution.py:193
  320.6 1.1 copy-done.4
  322.1 1.8 convolution_convert_fusion.5
  323.9 55.8 %reduce-scatter.11.cloned.1.call-done = bf16[64,6144]{1,0:T(8,128)(2,1)} async-done(((bf16[256,6144]{1,0:T(8,128)(2,1)}), bf16[64,6144]{1,0:T(8,128)(2,1)}) %reduce-scatter.11.cloned.1.call-update) | async-done | bytes 786448 | tf_op jit(solution)/shard_map/reduce_scatter | solution.py:173
  379.7 1.3 multiply_convert_fusion.1
  381.0 2.9 convolution_convert_fusion.4
  (49 shorter events, 3.0 us)
Async XLA Ops:
  7.2 117.6 %copy-start = (bf16[128,6144]{1,0:T(8,128)(2,1)S(1)}, bf16[128,6144]{1,0:T(8,128)(2,1)}, u32[]{:S(2)}) copy-start(bf16[128,6144]{1,0:T(8,128)(2,1)} %param.14) | copy-start | bytes 4718596
  7.2 24.5 %copy-start.9 = (s32[512,2]{0,1:T(2,128)S(1)}, s32[512,2]{0,1:T(2,128)}, u32[]{:S(2)}) copy-start(s32[512,2]{0,1:T(2,128)} %param.19) | copy-start | bytes 12292
  7.2 59.1 %all-gather.6.cloned.1.call-start = ((), (), s32[]{:S(2)}) async-start(), calls=%async_computation.8 | async-start | bytes 2621440 | tf_op jit(solution)/shard_map/all_gather | solution.py:126
  34.3 7.5 %copy-start.10 = (s32[4]{0:T(128)S(1)}, s32[4]{0:T(128)}, u32[]{:S(2)}) copy-start(s32[4]{0:T(128)} %param.18) | copy-start | bytes 52
  37.9 28.4 %all-to-all-start = ((bf16[128,4,1024]{2,0,1:T(8,128)(2,1)}), bf16[128,4,1024]{2,0,1:T(8,128)(2,1)S(1)}, u32[]{:S(2)}, u32[]{:S(2)}) async-start(bf16[128,4,1024]{2,0,1:T(8,128)(2,1)} %copy.22), calls=%async_computation.1 | async-start | bytes 2097152 | tf_op jit(solution)/shard_map/all_to_all | solution.py:152
  41.4 108.9 %reduce-scatter.9.cloned.1.call-start = ((), (), s32[]{:S(2)}) async-start(), calls=%async_computation.10 | async-start | bytes 3932160 | tf_op jit(solution)/shard_map/reduce_scatter | solution.py:173
  66.3 1.6 copy-start.2
  87.6 125.3 %reduce-scatter.7.cloned.1.call-start = ((), (), s32[]{:S(2)}) async-start(), calls=%async_computation.9 | async-start | bytes 3932160 | tf_op jit(solution)/shard_map/reduce_scatter | solution.py:173
  87.7 1.6 copy-start.3
  127.0 88.7 %copy-start.8 = (f32[6144]{0:T(1024)S(1)}, f32[6144]{0:T(1024)}, u32[]{:S(2)}) copy-start(f32[6144]{0:T(1024)} %param.21) | copy-start | bytes 73732
  127.0 89.8 %copy-start.7 = (bf16[6144,8]{0,1:T(8,128)(2,1)S(1)}, bf16[6144,8]{0,1:T(8,128)(2,1)}, u32[]{:S(2)}) copy-start(bf16[6144,8]{0,1:T(8,128)(2,1)} %param.22) | copy-start | bytes 294916
  217.1 79.7 %copy-start.6 = (bf16[64,6144]{1,0:T(8,128)(2,1)}, bf16[64,6144]{1,0:T(8,128)(2,1)S(1)}, u32[]{:S(2)}) copy-start(bf16[64,6144]{1,0:T(8,128)(2,1)S(1)} %get-tuple-element.44) | copy-start | bytes 2359300
  217.2 66.2 %all-gather.8.cloned.1.call-start = ((), (), s32[]{:S(2)}) async-start(), calls=%async_computation.11 | async-start | bytes 3932160 | tf_op jit(solution)/shard_map/all_gather | solution.py:183
  217.7 162.0 %reduce-scatter.11.cloned.1.call-start = ((), (), s32[]{:S(2)}) async-start(), calls=%async_computation.12 | async-start | bytes 3932160 | tf_op jit(solution)/shard_map/reduce_scatter | solution.py:173
  320.6 1.1 copy-start.4
  322.1 61.8 %copy-start.1 = (bf16[128,6144]{1,0:T(8,128)(2,1)S(1)}, bf16[128,6144]{1,0:T(8,128)(2,1)}, u32[]{:S(2)}) copy-start(bf16[128,6144]{1,0:T(8,128)(2,1)} %param.14) | copy-start | bytes 4718596
Sparse Core Ops, SparseCore 0:
  31.8 21.6 all-gather.5
  87.7 62.4 reduce-scatter.8
  152.6 60.2 reduce-scatter.6
  219.8 63.5 all-gather.7
  320.7 58.8 reduce-scatter.10
